TPU v7x, 32 devices: a whole 2x2x4 slice. The times are simulated.
32 devices in a mesh: clip: 4 (over y, x), seq: 8 (over z, core).
Axes of the slice: x: 2, y: 2, z: 4, core: 2. Of those that a mesh axis runs over, the one named last changes fastest.
Arguments:
- tokens: bfloat16 [81920, 1280], P(('clip', 'seq')), parts along dimension 0, may hold values from -6 to 6
- slot_proj: bfloat16 [1280, 16], replicated, may hold values from -5 to 5, as said below
- w_in: bfloat16 [8, 1280, 2560], P('seq'), may hold values from -0.15625 to 0.15625
- w_out: bfloat16 [8, 2560, 1280], P('seq'), may hold values from -0.125 to 0.125
Outputs:
- mixed: bfloat16 [81920, 1280], P(('clip', 'seq')), parts along dimension 0
There are 4 independent parts, one for each index of `clip`. A program takes and returns all parts, laid end to end along the dimension named above; an argument that names none is the same for every part. Nothing has to cross between parts.
Inputs may be any that keep to these rules, and one draw needn't show every extreme that they name: `slot_proj`: the slots' parameters.
All inputs are finite; a program needn't handle non-finite values.
Results may differ from a plain program's by a relative error of at most 0.02.
Values may be sent and summed in bfloat16 or wider, within the bound.
A program may use at most 64 MiB of HBM per device.

v0:
```python
import jax
import jax.numpy as jnp
from jax import lax
from jax.sharding import PartitionSpec as P

SLOTS = 2


def body(tokens, slot_proj, w_in, w_out):
    logits = jnp.dot(tokens, slot_proj, preferred_element_type=jnp.float32)
    own_rows = w_in.shape[0] * SLOTS
    start_row = lax.axis_index("seq") * own_rows
    width = tokens.shape[1]
    col_max = lax.pmax(jnp.max(logits, axis=0), "seq")
    shifted = jnp.exp(logits - col_max[None, :])
    dispatch = shifted.astype(jnp.bfloat16)
    part_total = jnp.sum(shifted, axis=0)
    col_total = lax.psum(part_total, "seq")
    full_num = lax.dot_general(
        dispatch, tokens, (((0,), (0,)), ((), ())), preferred_element_type=jnp.float32
    )
    num_all = lax.psum(full_num.astype(jnp.bfloat16), "seq").astype(jnp.float32)
    own_total = lax.dynamic_slice_in_dim(col_total, start_row, own_rows, 0)
    own_num = lax.dynamic_slice_in_dim(num_all, start_row, own_rows, 0)
    slot_in = (own_num / own_total[:, None]).astype(jnp.bfloat16)
    slot_in = slot_in.reshape(w_in.shape[0], SLOTS, width)
    hidden = jax.nn.gelu(
        jnp.einsum("esd,edf->esf", slot_in, w_in, preferred_element_type=jnp.float32)
    ).astype(jnp.bfloat16)
    slot_out = jnp.einsum("esf,efd->esd", hidden, w_out, preferred_element_type=jnp.float32).astype(
        jnp.bfloat16
    )
    slot_out = slot_out.reshape(own_rows, width)
    combine = jax.nn.softmax(logits, axis=1).astype(jnp.bfloat16)
    mixed = jnp.dot(
        combine,
        lax.all_gather(slot_out, "seq", axis=0, tiled=True),
        preferred_element_type=jnp.float32,
    )
    return mixed.astype(jnp.bfloat16)


def solution(mesh):
    return jax.shard_map(
        body,
        mesh=mesh,
        in_specs=(P(("clip", "seq"), None), P(), P("seq", None, None), P("seq", None, None)),
        out_specs=P(("clip", "seq"), None),
        check_vma=False,
    )
```

profile of v0, /device:TPU:0, one launch (start us, length us, event | category | flops | bytes accessed | tf_op | source)
XLA Modules:
  0.0 93.1 jit_solution(6319411518015298279)
XLA Ops:
  0.0 0.0 copy-start
  0.0 0.8 copy-done
  0.8 4.8 %fusion.48 = (f32[2560]{0:T(1024)S(1)}, f32[16]{0:T(128)S(1)}, f32[2560,16]{0,1:T(8,128)S(1)}) fusion(bf16[2560,1280]{1,0:T(8,128)(2,1)} %param.4, bf16[1280,16]{0,1:T(8,128)(2,1)S(1)} %copy-done), kind=kOutput, calls=%fused_computation.39 | convolution fusion | flops 104936944 | bytes 6768704 | tf_op jit(solution)/shard_map/dot_general | solution.py:10
  5.6 18.1 %pmax.7 = f32[16]{0:T(128)S(1)} all-reduce(f32[16]{0:T(128)S(1)} %get-tuple-element.8), channel_id=1, replica_groups=mesh['clip'=4,'seq'=8] {'seq'}, use_global_device_ids=true, to_apply=%region_3.0 | all-reduce | flops 16 | bytes 128 | tf_op jit(solution)/shard_map/pmax | solution.py:14
  23.6 0.2 fusion.10
  23.8 13.6 %psum.15 = f32[16]{0:T(128)S(1)} all-reduce(f32[16]{0:T(128)S(1)} %get-tuple-element.6), channel_id=1, replica_groups=mesh['clip'=4,'seq'=8] {'seq'}, use_global_device_ids=true, to_apply=%region_6.0 | all-reduce | flops 16 | bytes 128 | tf_op jit(solution)/shard_map/psum | solution.py:18
  37.4 0.1 dynamic_slice.7
  37.5 3.9 %convolution_convert_fusion.1 = bf16[16,1280]{1,0:T(8,128)(2,1)S(1)} fusion(bf16[2560,1280]{1,0:T(8,128)(2,1)} %param.4, f32[2560,16]{0,1:T(8,128)S(1)} %get-tuple-element.9, f32[16]{0:T(128)S(1)} %pmax.7), kind=kOutput, calls=%fused_computation.5 | convolution fusion | flops 104960000 | bytes 6758464 | tf_op jit(solution)/shard_map/dot_general | solution.py:19
  41.4 26.3 %psum.14 = bf16[16,1280]{1,0:T(8,128)(2,1)S(1)} all-reduce(bf16[16,1280]{1,0:T(8,128)(2,1)S(1)} %convolution_convert_fusion.1), channel_id=1, replica_groups=mesh['clip'=4,'seq'=8] {'seq'}, use_global_device_ids=true, to_apply=%region_4.0 | all-reduce | flops 20480 | bytes 81920 | tf_op jit(solution)/shard_map/psum | solution.py:22
  67.7 6.7 %fusion.7 = bf16[1,2,1280]{2,1,0:T(2,128)(2,1)S(1)} fusion(bf16[1,2560,1280]{2,1,0:T(8,128)(2,1)} %param.7, bf16[1,1280,2560]{2,1,0:T(8,128)(2,1)} %param.6, f32[2]{0:T(128)S(1)} %dynamic_slice.7, bf16[16,1280]{1,0:T(8,128)(2,1)S(1)} %psum.14, s32[]{:T(128)S(6)} %select_n.4), kind=kOutput, calls=%fused_computation.7 | convolution fusion | flops 26270720 | bytes 13117956 | tf_op jit(solution)/shard_map/esf,efd->esd/dot_general | solution.py:30
  74.4 14.0 %all-gather = bf16[8,2,1280]{2,1,0:T(2,128)(2,1)S(1)} all-gather(bf16[1,2,1280]{2,1,0:T(2,128)(2,1)S(1)} %fusion.7), channel_id=1, replica_groups=mesh['clip'=4,'seq'=8] {'seq'}, dimensions={0}, use_global_device_ids=true | all-gather | bytes 46080 | tf_op jit(solution)/shard_map/all_gather | solution.py:37
  88.4 4.7 %convolution_convert_fusion = bf16[2560,1280]{1,0:T(8,128)(2,1)} fusion(bf16[16,1280]{1,0:T(8,128)(2,1)S(1)} %reshape.33, f32[2560,16]{0,1:T(8,128)S(1)} %get-tuple-element.9, f32[2560]{0:T(1024)S(1)} %get-tuple-element.5, f32[2560]{0:T(1024)S(1)} %get-tuple-element.7), kind=kOutput, calls=%fused_computation | convolution fusion | flops 108257280 | bytes 6778880 | tf_op jit(solution)/shard_map/dot_general | solution.py:35
  (1 shorter events, 0.0 us)
Async XLA Ops:
  0.0 0.8 copy-start
where the time goes:
time: 93.4 us; the launch traced here: 93.1 us
  blocking collectives  72 us (77%)
  matrix products  20.1 us (22%)
    psum x1, blocking collectives, body(): num_all = lax.psum(full_num.astype(jnp.bfloat16), 'seq').astype(jnp.float32)  26.3 us
    pmax x1, blocking collectives, body(): col_max = lax.pmax(jnp.max(logits, axis=0), 'seq')  18.1 us
    all_gather x1, blocking collectives, body(): lax.all_gather(slot_out, 'seq', axis=0, tiled=True)  14 us
    psum x1, blocking collectives, body(): col_total = lax.psum(part_total, 'seq')  13.6 us
    dot_general x1, matrix products, body(): jnp.einsum('esf,efd->esd', hidden, w_out, preferred_element_type=jnp.floa...  6.7 us
    dot_general x1, matrix products, body(): logits = jnp.dot(tokens, slot_proj, preferred_element_type=jnp.float32)  4.78 us
    dot_general x1, matrix products, body(): jnp.dot(combine, lax.all_gather(slot_out, 'seq', axis=0, tiled=True), pre...  4.71 us
    dot_general x1, matrix products, body(): lax.dot_general(dispatch, tokens, (((0,), (0,)), ((), ())), preferred_ele...  3.86 us

commit v1 on v0

v1 whole, which is shorter than its diff:
```python
import functools

import jax
import jax.numpy as jnp
from jax import lax
from jax.experimental import pallas as pl
from jax.experimental.pallas import tpu as pltpu
from jax.sharding import PartitionSpec as P

MESH = pl.DeviceIdType.MESH
F32 = jnp.float32
BF16 = jnp.bfloat16
TOKEN_PARTS = 5
FF_PARTS = 4
STAT = 128


def route_kernel(
    n,
    tokens_hbm,
    proj_hbm,
    w_in_hbm,
    w_out_hbm,
    combine_ref,
    slots_ref,
    tok,
    proj,
    w_in,
    w_out,
    logits,
    send,
    recv,
    gather,
    rows,
    tok_sem,
    proj_sem,
    in_sem,
    out_sem,
    s1_sem,
    r1_sem,
    s2_sem,
    r2_sem,
):
    me = lax.axis_index("seq")
    width = tok.shape[1]
    slots = send.shape[1]
    part = tok.shape[0] // TOKEN_PARTS
    ff = w_in.shape[1]
    ff_part = ff // FF_PARTS

    proj_copy = pltpu.make_async_copy(proj_hbm, proj, proj_sem)
    proj_copy.start()
    tok_copies = []
    for c in range(TOKEN_PARTS):
        at = pl.ds(c * part, part)
        copy = pltpu.make_async_copy(tokens_hbm.at[at, :], tok.at[at, :], tok_sem.at[c])
        copy.start()
        tok_copies.append(copy)
    in_copies, out_copies = [], []
    for c in range(FF_PARTS):
        at = pl.ds(c * ff_part, ff_part)
        copy = pltpu.make_async_copy(w_in_hbm.at[0, :, at], w_in.at[:, at], in_sem.at[c])
        copy.start()
        in_copies.append(copy)
        copy = pltpu.make_async_copy(w_out_hbm.at[0, at, :], w_out.at[at, :], out_sem.at[c])
        copy.start()
        out_copies.append(copy)

    barrier = pltpu.get_barrier_semaphore()
    peers = [lax.rem(me + off, n) for off in range(1, n)]
    for peer in peers:
        pl.semaphore_signal(barrier, inc=1, device_id={"seq": peer}, device_id_type=MESH)

    proj_copy.wait()
    proj_cols = proj[...].T
    top = total = num = None
    for c in range(TOKEN_PARTS):
        tok_copies[c].wait()
        x = tok[c * part : (c + 1) * part, :]
        l = jnp.dot(x, proj_cols, preferred_element_type=F32).T
        logits[:, c * part : (c + 1) * part] = l
        here = jnp.max(l, axis=1, keepdims=True)
        new = here if c == 0 else jnp.maximum(top, here)
        shifted = jnp.exp(l - new)
        t = jnp.sum(shifted, axis=1, keepdims=True)
        v = jnp.dot(shifted.astype(BF16), x, preferred_element_type=F32)
        if c == 0:
            total, num = t, v
        else:
            keep = jnp.exp(top - new)
            total, num = total * keep + t, num * keep + v
        top = new

    for e in range(n):
        at = slice(e * slots, (e + 1) * slots)
        send[e, :, :width] = num[at, :]
        send[e, :, width : width + STAT] = jnp.broadcast_to(top[at, :], (slots, STAT))
        send[e, :, width + STAT :] = jnp.broadcast_to(total[at, :], (slots, STAT))

    pl.semaphore_wait(barrier, n - 1)
    first = []
    for k, peer in enumerate(peers):
        copy = pltpu.make_async_remote_copy(
            src_ref=send.at[peer],
            dst_ref=recv.at[k],
            send_sem=s1_sem.at[k],
            recv_sem=r1_sem.at[k],
            device_id={"seq": peer},
            device_id_type=MESH,
        )
        copy.start()
        first.append(copy)

    l = logits[...]
    e = jnp.exp(l - jnp.max(l, axis=0, keepdims=True))
    combine_ref[...] = (e / jnp.sum(e, axis=0, keepdims=True)).astype(BF16)

    for copy in first:
        copy.wait_recv()
    own = send[me]
    tops = [own[:, width : width + STAT]] + [recv[k, :, width : width + STAT] for k in range(n - 1)]
    top = functools.reduce(jnp.maximum, tops)
    total = jnp.zeros((slots, STAT), F32)
    num = jnp.zeros((slots, width), F32)
    for k in range(n):
        scale = jnp.exp(tops[k] - top)
        got = own if k == 0 else recv[k - 1]
        total = total + scale * got[:, width + STAT :]
        num = num + scale[:, :1] * got[:, :width]
    slot_in = (num / total[:, :1]).astype(BF16)

    slot_out = jnp.zeros((slots, width), F32)
    for c in range(FF_PARTS):
        at = slice(c * ff_part, (c + 1) * ff_part)
        in_copies[c].wait()
        hidden = jnp.dot(slot_in, w_in[:, at], preferred_element_type=F32)
        hidden = jax.nn.gelu(hidden).astype(BF16)
        out_copies[c].wait()
        slot_out = slot_out + jnp.dot(hidden, w_out[at, :], preferred_element_type=F32)
    gather[me] = slot_out.astype(BF16).astype(F32)

    second = []
    for k, peer in enumerate(peers):
        copy = pltpu.make_async_remote_copy(
            src_ref=gather.at[me],
            dst_ref=gather.at[me],
            send_sem=s2_sem.at[k],
            recv_sem=r2_sem.at[k],
            device_id={"seq": peer},
            device_id_type=MESH,
        )
        copy.start()
        second.append(copy)
    for copy in second:
        copy.wait_recv()
    for e in range(n):
        rows[e * slots : (e + 1) * slots, :] = gather[e]
    slots_ref[...] = rows[...].astype(BF16)
    for copy in first + second:
        copy.wait_send()


def mix_kernel(combine_ref, slots_ref, out_ref):
    out_ref[...] = lax.dot_general(
        combine_ref[...], slots_ref[...], (((0,), (0,)), ((), ())), preferred_element_type=F32
    ).astype(BF16)


def body(n, tokens, slot_proj, w_in, w_out):
    count, width = tokens.shape
    slots_all = slot_proj.shape[1]
    slots = slots_all // n
    ff = w_in.shape[2]
    assert w_in.shape[0] == 1
    any_spec = pl.BlockSpec(memory_space=pl.ANY)
    vmem_spec = pl.BlockSpec(memory_space=pltpu.VMEM)
    wide = width + 2 * STAT
    dma = pltpu.SemaphoreType.DMA
    combine, slot_out = pl.pallas_call(
        functools.partial(route_kernel, n),
        out_shape=[
            jax.ShapeDtypeStruct((slots_all, count), BF16),
            jax.ShapeDtypeStruct((slots_all, width), BF16),
        ],
        in_specs=[any_spec] * 4,
        out_specs=[vmem_spec] * 2,
        scratch_shapes=[
            pltpu.VMEM((count, width), BF16),
            pltpu.VMEM((slots_all, width), BF16),
            pltpu.VMEM((width, ff), BF16),
            pltpu.VMEM((ff, width), BF16),
            pltpu.VMEM((slots_all, count), F32),
            pltpu.VMEM((n, slots, wide), F32),
            pltpu.VMEM((n - 1, slots, wide), F32),
            pltpu.VMEM((n, slots, width), F32),
            pltpu.VMEM((slots_all, width), F32),
            dma((TOKEN_PARTS,)),
            dma,
            dma((FF_PARTS,)),
            dma((FF_PARTS,)),
            dma((n - 1,)),
            dma((n - 1,)),
            dma((n - 1,)),
            dma((n - 1,)),
        ],
        compiler_params=pltpu.CompilerParams(
            collective_id=0, has_side_effects=True, vmem_limit_bytes=48 * 1024 * 1024
        ),
        cost_estimate=pl.CostEstimate(
            flops=4 * count * width * slots_all + 4 * slots * width * ff,
            bytes_accessed=2 * (count * width + 2 * width * ff),
            transcendentals=2 * count * slots_all,
        ),
        name="route",
    )(tokens, slot_proj.T, w_in, w_out)
    part = count // TOKEN_PARTS
    return pl.pallas_call(
        mix_kernel,
        grid=(TOKEN_PARTS,),
        out_shape=jax.ShapeDtypeStruct((count, width), BF16),
        in_specs=[
            pl.BlockSpec((slots_all, part), lambda i: (0, i)),
            pl.BlockSpec((slots_all, width), lambda i: (0, 0)),
        ],
        out_specs=pl.BlockSpec((part, width), lambda i: (i, 0)),
        compiler_params=pltpu.CompilerParams(vmem_limit_bytes=32 * 1024 * 1024),
        cost_estimate=pl.CostEstimate(
            flops=2 * count * width * slots_all,
            bytes_accessed=2 * count * width,
            transcendentals=0,
        ),
        name="mix",
    )(combine, slot_out)


def solution(mesh):
    return jax.shard_map(
        functools.partial(body, mesh.shape["seq"]),
        mesh=mesh,
        in_specs=(P(("clip", "seq"), None), P(), P("seq", None, None), P("seq", None, None)),
        out_specs=P(("clip", "seq"), None),
        check_vma=False,
    )
```

time: 93.4 us -> 27 us (0.29)
  blocking collectives: 72 us -> 0 us
  Pallas kernels: 0 us -> 26.1 us
  matrix products: 20.1 us -> 0 us
    psum x2 -> x0, blocking collectives: 39.9 us -> none  [the longest x1 26.3 us: body(): num_all = lax.psum(full_num.astype(jnp.bfloat16), 'seq').astype(jnp.float32)]
    pallas_call x0 -> x2, Pallas kernels: none -> 26.1 us  [the longest x1 21.3 us: body(): pl.pallas_call(functools.partial(route_kernel, n), out_shape=[jax.ShapeDt...]
    dot_general x4 -> x0, matrix products: 20.1 us -> none  [the longest x1 6.7 us: body(): jnp.einsum('esf,efd->esd', hidden, w_out, preferred_element_type=jnp.floa...]
    pmax x1 -> x0, blocking collectives: 18.1 us -> none  [body(): col_max = lax.pmax(jnp.max(logits, axis=0), 'seq')]
    all_gather x1 -> x0, blocking collectives: 14 us -> none  [body(): lax.all_gather(slot_out, 'seq', axis=0, tiled=True)]
where the time goes in v1:
time: 27 us; the launch traced here: 26.9 us
  Pallas kernels  26.1 us (97%)
  local copies, waits for them, and re-layouts  0.78 us (3%)
    pallas_call x1, Pallas kernels, body(): pl.pallas_call(functools.partial(route_kernel, n), out_shape=[jax.ShapeDt...  21.3 us
    pallas_call x1, Pallas kernels, body(): pl.pallas_call(mix_kernel, grid=(TOKEN_PARTS,), out_shape=jax.ShapeDtypeS...  4.8 us
    unnamed x2, local copies, waits for them, and re-layouts  0.78 us

profile of v1, /device:TPU:0, one launch (start us, length us, event | category | flops | bytes accessed | tf_op | source)
XLA Modules:
  0.0 26.9 jit_solution(3655839183740381362)
XLA Ops:
  0.0 0.0 copy-start
  0.0 0.8 %copy-done = bf16[1280,16]{0,1:T(8,128)(2,1)S(1)} copy-done((bf16[1280,16]{0,1:T(8,128)(2,1)S(1)}, bf16[1280,16]{0,1:T(8,128)(2,1)}, u32[]{:S(2)}) %copy-start) | copy-done | bytes 40984
  0.8 21.3 %route.1 = (bf16[16,2560]{1,0:T(8,128)(2,1)S(1)}, bf16[16,1280]{1,0:T(8,128)(2,1)S(1)}) custom-call(bf16[2560,1280]{1,0:T(8,128)(2,1)} %tokens_hbm.1, bf16[16,1280]{1,0:T(8,128)(2,1)S(1)} %bitcast.1, bf16[1,1280,2560]{2,1,0:T(8,128)(2,1)} %w_in_hbm.1, bf16[1,2560,1280]{2,1,0:T(8,128)(2,1)} %w_out_hbm.1), custom_call_target="tpu_custom_call" | custom-call | flops 235929600 | bytes 19660800 | tf_op jit(solution)/shard_map/route/pallas_call | solution.py:179
  22.1 4.8 %mix.1 = bf16[2560,1280]{1,0:T(8,128)(2,1)} custom-call(bf16[16,2560]{1,0:T(8,128)(2,1)S(1)} %get-tuple-element.7.combine_ref, bf16[16,1280]{1,0:T(8,128)(2,1)S(1)} %get-tuple-element.8.slots_ref), custom_call_target="tpu_custom_call" | custom-call | flops 104857600 | bytes 6553600 | tf_op jit(solution)/shard_map/mix/pallas_call | solution.py:217
Async XLA Ops:
  0.0 0.8 %copy-start = (bf16[1280,16]{0,1:T(8,128)(2,1)S(1)}, bf16[1280,16]{0,1:T(8,128)(2,1)}, u32[]{:S(2)}) copy-start(bf16[1280,16]{0,1:T(8,128)(2,1)} %param.5) | copy-start | bytes 122884

commit v2 on v1

--- a/solution.py
+++ b/solution.py
@@ -12,6 +12,7 @@
 BF16 = jnp.bfloat16
 TOKEN_PARTS = 5
 FF_PARTS = 4
+MIX_PARTS = 10
 STAT = 128
 
 
@@ -59,12 +60,8 @@
     in_copies, out_copies = [], []
     for c in range(FF_PARTS):
         at = pl.ds(c * ff_part, ff_part)
-        copy = pltpu.make_async_copy(w_in_hbm.at[0, :, at], w_in.at[:, at], in_sem.at[c])
-        copy.start()
-        in_copies.append(copy)
-        copy = pltpu.make_async_copy(w_out_hbm.at[0, at, :], w_out.at[at, :], out_sem.at[c])
-        copy.start()
-        out_copies.append(copy)
+        in_copies.append(pltpu.make_async_copy(w_in_hbm.at[0, :, at], w_in.at[:, at], in_sem.at[c]))
+        out_copies.append(pltpu.make_async_copy(w_out_hbm.at[0, at, :], w_out.at[at, :], out_sem.at[c]))
 
     barrier = pltpu.get_barrier_semaphore()
     peers = [lax.rem(me + off, n) for off in range(1, n)]
@@ -73,23 +70,34 @@
 
     proj_copy.wait()
     proj_cols = proj[...].T
+
+    def part_logits(c):
+        tok_copies[c].wait()
+        at = slice(c * part, (c + 1) * part)
+        l = jnp.dot(tok[at, :], proj_cols, preferred_element_type=F32).T
+        logits[:, at] = l
+        return l
+
     top = total = num = None
+    l = part_logits(0)
     for c in range(TOKEN_PARTS):
-        tok_copies[c].wait()
-        x = tok[c * part : (c + 1) * part, :]
-        l = jnp.dot(x, proj_cols, preferred_element_type=F32).T
-        logits[:, c * part : (c + 1) * part] = l
+        if c + 1 < TOKEN_PARTS:
+            following = part_logits(c + 1)
+            if c + 2 == TOKEN_PARTS:
+                for copy in in_copies + out_copies:
+                    copy.start()
         here = jnp.max(l, axis=1, keepdims=True)
         new = here if c == 0 else jnp.maximum(top, here)
         shifted = jnp.exp(l - new)
         t = jnp.sum(shifted, axis=1, keepdims=True)
+        x = tok[c * part : (c + 1) * part, :]
         v = jnp.dot(shifted.astype(BF16), x, preferred_element_type=F32)
         if c == 0:
             total, num = t, v
         else:
             keep = jnp.exp(top - new)
             total, num = total * keep + t, num * keep + v
-        top = new
+        top, l = new, following
 
     for e in range(n):
         at = slice(e * slots, (e + 1) * slots)
@@ -113,7 +121,7 @@
 
     l = logits[...]
     e = jnp.exp(l - jnp.max(l, axis=0, keepdims=True))
-    combine_ref[...] = (e / jnp.sum(e, axis=0, keepdims=True)).astype(BF16)
+    combine_ref[...] = (e / jnp.sum(e, axis=0, keepdims=True)).T.astype(BF16)
 
     for copy in first:
         copy.wait_recv()
@@ -129,13 +137,13 @@
         num = num + scale[:, :1] * got[:, :width]
     slot_in = (num / total[:, :1]).astype(BF16)
 
+    for copy in in_copies + out_copies:
+        copy.wait()
     slot_out = jnp.zeros((slots, width), F32)
     for c in range(FF_PARTS):
         at = slice(c * ff_part, (c + 1) * ff_part)
-        in_copies[c].wait()
         hidden = jnp.dot(slot_in, w_in[:, at], preferred_element_type=F32)
         hidden = jax.nn.gelu(hidden).astype(BF16)
-        out_copies[c].wait()
         slot_out = slot_out + jnp.dot(hidden, w_out[at, :], preferred_element_type=F32)
     gather[me] = slot_out.astype(BF16).astype(F32)
 
@@ -160,10 +168,19 @@
         copy.wait_send()
 
 
-def mix_kernel(combine_ref, slots_ref, out_ref):
-    out_ref[...] = lax.dot_general(
-        combine_ref[...], slots_ref[...], (((0,), (0,)), ((), ())), preferred_element_type=F32
-    ).astype(BF16)
+def mix_kernel(combine_ref, slots_ref, out_hbm, out, out_sem):
+    part = out.shape[0] // MIX_PARTS
+    copies = []
+    for c in range(MIX_PARTS):
+        at = pl.ds(c * part, part)
+        out[at, :] = jnp.dot(
+            combine_ref[at, :], slots_ref[...], preferred_element_type=F32
+        ).astype(BF16)
+        copy = pltpu.make_async_copy(out.at[at, :], out_hbm.at[at, :], out_sem.at[c])
+        copy.start()
+        copies.append(copy)
+    for copy in copies:
+        copy.wait()
 
 
 def body(n, tokens, slot_proj, w_in, w_out):
@@ -172,17 +189,17 @@
     slots = slots_all // n
     ff = w_in.shape[2]
     assert w_in.shape[0] == 1
-    any_spec = pl.BlockSpec(memory_space=pl.ANY)
+    hbm_spec = pl.BlockSpec(memory_space=pltpu.HBM)
     vmem_spec = pl.BlockSpec(memory_space=pltpu.VMEM)
     wide = width + 2 * STAT
     dma = pltpu.SemaphoreType.DMA
     combine, slot_out = pl.pallas_call(
         functools.partial(route_kernel, n),
         out_shape=[
-            jax.ShapeDtypeStruct((slots_all, count), BF16),
+            jax.ShapeDtypeStruct((count, slots_all), BF16),
             jax.ShapeDtypeStruct((slots_all, width), BF16),
         ],
-        in_specs=[any_spec] * 4,
+        in_specs=[hbm_spec] * 4,
         out_specs=[vmem_spec] * 2,
         scratch_shapes=[
             pltpu.VMEM((count, width), BF16),
@@ -212,17 +229,13 @@
             transcendentals=2 * count * slots_all,
         ),
         name="route",
-    )(tokens, slot_proj.T, w_in, w_out)
-    part = count // TOKEN_PARTS
+    )(tokens, pltpu.with_memory_space_constraint(slot_proj.T, pltpu.HBM), w_in, w_out)
     return pl.pallas_call(
         mix_kernel,
-        grid=(TOKEN_PARTS,),
         out_shape=jax.ShapeDtypeStruct((count, width), BF16),
-        in_specs=[
-            pl.BlockSpec((slots_all, part), lambda i: (0, i)),
-            pl.BlockSpec((slots_all, width), lambda i: (0, 0)),
-        ],
-        out_specs=pl.BlockSpec((part, width), lambda i: (i, 0)),
+        in_specs=[vmem_spec] * 2,
+        out_specs=hbm_spec,
+        scratch_shapes=[pltpu.VMEM((count, width), BF16), dma((MIX_PARTS,))],
         compiler_params=pltpu.CompilerParams(vmem_limit_bytes=32 * 1024 * 1024),
         cost_estimate=pl.CostEstimate(
             flops=2 * count * width * slots_all,

time: 27 us -> 23.1 us (0.86)
  Pallas kernels: 26.1 us -> 22.9 us
  local copies, waits for them, and re-layouts: 0.78 us -> 0 us
    pallas_call x1, Pallas kernels: 4.8 us -> 3.16 us  [body(): pl.pallas_call(mix_kernel, out_shape=jax.ShapeDtypeStruct((count, width),...]
    pallas_call x1, Pallas kernels: 21.3 us -> 19.7 us  [body(): pl.pallas_call(functools.partial(route_kernel, n), out_shape=[jax.ShapeDt...]
    unnamed x2 -> x0, local copies, waits for them, and re-layouts: 0.78 us -> none
where the time goes in v2:
time: 23.1 us; the launch traced here: 22.9 us
  Pallas kernels  22.9 us (99%)
    pallas_call x1, Pallas kernels, body(): pl.pallas_call(functools.partial(route_kernel, n), out_shape=[jax.ShapeDt...  19.7 us
    pallas_call x1, Pallas kernels, body(): pl.pallas_call(mix_kernel, out_shape=jax.ShapeDtypeStruct((count, width),...  3.16 us

profile of v2, /device:TPU:0, one launch (start us, length us, event | category | flops | bytes accessed | tf_op | source)
XLA Modules:
  0.0 22.9 jit_solution(7191914400751882073)
XLA Ops:
  0.0 19.7 %route.1 = (bf16[2560,16]{1,0:T(8,128)(2,1)S(1)}, bf16[16,1280]{1,0:T(8,128)(2,1)S(1)}) custom-call(bf16[2560,1280]{1,0:T(8,128)(2,1)} %tokens_hbm.1, bf16[16,1280]{1,0:T(8,128)(2,1)} %bitcast.1, bf16[1,1280,2560]{2,1,0:T(8,128)(2,1)} %w_in_hbm.1, bf16[1,2560,1280]{2,1,0:T(8,128)(2,1)} %w_out_hbm.1), custom_call_target="tpu_custom_call" | custom-call | flops 235929600 | bytes 19660800 | tf_op jit(solution)/shard_map/route/pallas_call | solution.py:196
  19.7 3.2 %mix.1 = bf16[2560,1280]{1,0:T(8,128)(2,1)} custom-call(bf16[2560,16]{1,0:T(8,128)(2,1)S(1)} %get-tuple-element.7.combine_ref, bf16[16,1280]{1,0:T(8,128)(2,1)S(1)} %get-tuple-element.8.slots_ref), custom_call_target="tpu_custom_call" | custom-call | flops 104857600 | bytes 6553600 | tf_op jit(solution)/shard_map/mix/pallas_call | solution.py:233

commit v3 on v2

--- a/solution.py
+++ b/solution.py
@@ -11,9 +11,15 @@
 F32 = jnp.float32
 BF16 = jnp.bfloat16
 TOKEN_PARTS = 5
-FF_PARTS = 4
+FF_PARTS = 5
 MIX_PARTS = 10
 STAT = 128
+
+
+def split3(x):
+    high = x.astype(BF16).astype(F32)
+    middle = (x - high).astype(BF16).astype(F32)
+    return [high, middle, x - high - middle]
 
 
 def route_kernel(
@@ -64,7 +70,7 @@
         out_copies.append(pltpu.make_async_copy(w_out_hbm.at[0, at, :], w_out.at[at, :], out_sem.at[c]))
 
     barrier = pltpu.get_barrier_semaphore()
-    peers = [lax.rem(me + off, n) for off in range(1, n)]
+    peers = [lax.bitwise_xor(me, n - 1 - k) for k in range(n - 1)]
     for peer in peers:
         pl.semaphore_signal(barrier, inc=1, device_id={"seq": peer}, device_id_type=MESH)
 
@@ -99,11 +105,14 @@
             total, num = total * keep + t, num * keep + v
         top, l = new, following
 
+    lane = lax.broadcasted_iota(jnp.int32, (num.shape[0], STAT), 1)
+    stats = jnp.zeros((num.shape[0], STAT), F32)
+    for i, term in enumerate(split3(top) + split3(total)):
+        stats = jnp.where(lane == i, term, stats)
     for e in range(n):
         at = slice(e * slots, (e + 1) * slots)
-        send[e, :, :width] = num[at, :]
-        send[e, :, width : width + STAT] = jnp.broadcast_to(top[at, :], (slots, STAT))
-        send[e, :, width + STAT :] = jnp.broadcast_to(total[at, :], (slots, STAT))
+        send[e, :, :width] = num[at, :].astype(BF16)
+        send[e, :, width:] = stats[at, :].astype(BF16)
 
     pl.semaphore_wait(barrier, n - 1)
     first = []
@@ -125,17 +134,17 @@
 
     for copy in first:
         copy.wait_recv()
-    own = send[me]
-    tops = [own[:, width : width + STAT]] + [recv[k, :, width : width + STAT] for k in range(n - 1)]
+    got = [send[me].astype(F32)] + [recv[k].astype(F32) for k in range(n - 1)]
+    terms = [[g[:, width + i : width + i + 1] for i in range(6)] for g in got]
+    tops = [t[0] + t[1] + t[2] for t in terms]
     top = functools.reduce(jnp.maximum, tops)
-    total = jnp.zeros((slots, STAT), F32)
+    total = jnp.zeros((slots, 1), F32)
     num = jnp.zeros((slots, width), F32)
     for k in range(n):
         scale = jnp.exp(tops[k] - top)
-        got = own if k == 0 else recv[k - 1]
-        total = total + scale * got[:, width + STAT :]
-        num = num + scale[:, :1] * got[:, :width]
-    slot_in = (num / total[:, :1]).astype(BF16)
+        total = total + scale * (terms[k][3] + terms[k][4] + terms[k][5])
+        num = num + scale * got[k][:, :width]
+    slot_in = (num / total).astype(BF16)
 
     for copy in in_copies + out_copies:
         copy.wait()
@@ -145,7 +154,7 @@
         hidden = jnp.dot(slot_in, w_in[:, at], preferred_element_type=F32)
         hidden = jax.nn.gelu(hidden).astype(BF16)
         slot_out = slot_out + jnp.dot(hidden, w_out[at, :], preferred_element_type=F32)
-    gather[me] = slot_out.astype(BF16).astype(F32)
+    gather[me] = slot_out.astype(BF16)
 
     second = []
     for k, peer in enumerate(peers):
@@ -162,7 +171,7 @@
     for copy in second:
         copy.wait_recv()
     for e in range(n):
-        rows[e * slots : (e + 1) * slots, :] = gather[e]
+        rows[e * slots : (e + 1) * slots, :] = gather[e].astype(F32)
     slots_ref[...] = rows[...].astype(BF16)
     for copy in first + second:
         copy.wait_send()
@@ -188,10 +197,10 @@
     slots_all = slot_proj.shape[1]
     slots = slots_all // n
     ff = w_in.shape[2]
-    assert w_in.shape[0] == 1
+    assert w_in.shape[0] == 1 and n & (n - 1) == 0
     hbm_spec = pl.BlockSpec(memory_space=pltpu.HBM)
     vmem_spec = pl.BlockSpec(memory_space=pltpu.VMEM)
-    wide = width + 2 * STAT
+    wide = width + STAT
     dma = pltpu.SemaphoreType.DMA
     combine, slot_out = pl.pallas_call(
         functools.partial(route_kernel, n),
@@ -207,9 +216,9 @@
             pltpu.VMEM((width, ff), BF16),
             pltpu.VMEM((ff, width), BF16),
             pltpu.VMEM((slots_all, count), F32),
-            pltpu.VMEM((n, slots, wide), F32),
-            pltpu.VMEM((n - 1, slots, wide), F32),
-            pltpu.VMEM((n, slots, width), F32),
+            pltpu.VMEM((n, slots, wide), BF16),
+            pltpu.VMEM((n - 1, slots, wide), BF16),
+            pltpu.VMEM((n, slots, width), BF16),
             pltpu.VMEM((slots_all, width), F32),
             dma((TOKEN_PARTS,)),
             dma,

time: 23.1 us -> 23.4 us (1.013)
  Pallas kernels: 22.9 us -> 23.2 us
    pallas_call x1, Pallas kernels: 19.7 us -> 20.1 us  [body(): pl.pallas_call(functools.partial(route_kernel, n), out_shape=[jax.ShapeDt...]
where the time goes in v3:
time: 23.4 us; the launch traced here: 23.2 us
  Pallas kernels  23.2 us (99%)
    pallas_call x1, Pallas kernels, body(): pl.pallas_call(functools.partial(route_kernel, n), out_shape=[jax.ShapeDt...  20.1 us
    pallas_call x1, Pallas kernels, body(): pl.pallas_call(mix_kernel, out_shape=jax.ShapeDtypeStruct((count, width),...  3.16 us

profile of v3, /device:TPU:0, one launch (start us, length us, event | category | flops | bytes accessed | tf_op | source)
XLA Modules:
  0.0 23.2 jit_solution(15122727091731742597)
XLA Ops:
  0.0 20.1 %route.1 = (bf16[2560,16]{1,0:T(8,128)(2,1)S(1)}, bf16[16,1280]{1,0:T(8,128)(2,1)S(1)}) custom-call(bf16[2560,1280]{1,0:T(8,128)(2,1)} %tokens_hbm.1, bf16[16,1280]{1,0:T(8,128)(2,1)} %bitcast.1, bf16[1,1280,2560]{2,1,0:T(8,128)(2,1)} %w_in_hbm.1, bf16[1,2560,1280]{2,1,0:T(8,128)(2,1)} %w_out_hbm.1), custom_call_target="tpu_custom_call" | custom-call | flops 235929600 | bytes 19660800 | tf_op jit(solution)/shard_map/route/pallas_call | solution.py:205
  20.1 3.2 %mix.1 = bf16[2560,1280]{1,0:T(8,128)(2,1)} custom-call(bf16[2560,16]{1,0:T(8,128)(2,1)S(1)} %get-tuple-element.7.combine_ref, bf16[16,1280]{1,0:T(8,128)(2,1)S(1)} %get-tuple-element.8.slots_ref), custom_call_target="tpu_custom_call" | custom-call | flops 104857600 | bytes 6553600 | tf_op jit(solution)/shard_map/mix/pallas_call | solution.py:242

commit v4 on v3

--- a/solution.py
+++ b/solution.py
@@ -13,6 +13,7 @@
 TOKEN_PARTS = 5
 FF_PARTS = 5
 MIX_PARTS = 10
+GROUP = 256
 STAT = 128
 
 
@@ -20,6 +21,28 @@
     high = x.astype(BF16).astype(F32)
     middle = (x - high).astype(BF16).astype(F32)
     return [high, middle, x - high - middle]
+
+
+def spread_slots(spread, x):
+    slots, depth = x.shape
+    columns = jnp.concatenate([x] * (8 // slots), axis=0).T
+    for i in range(slots):
+        spread[i, :depth, :] = jnp.broadcast_to(columns[:, i : i + 1], (depth, 128)).astype(BF16)
+
+
+def vector_dot(spread, w, row, depth, column):
+    slots = spread.shape[0]
+    sums = [jnp.zeros((16, GROUP), F32) for _ in range(slots)]
+    for d in range(0, depth, 64):
+        tiles = [w[row + d + r : row + d + r + 16, column : column + GROUP] for r in range(0, 64, 16)]
+        for i in range(slots):
+            terms = []
+            for k, tile in enumerate(tiles):
+                value = spread[i, d + 16 * k : d + 16 * k + 16, :]
+                terms.append(tile * jnp.concatenate([value] * (GROUP // 128), axis=1))
+            pair = (terms[0] + terms[1]) + (terms[2] + terms[3])
+            sums[i] = sums[i] + pair.astype(F32)
+    return jnp.concatenate([jnp.sum(x, axis=0, keepdims=True) for x in sums], axis=0)
 
 
 def route_kernel(
@@ -39,6 +62,7 @@
     recv,
     gather,
     rows,
+    spread,
     tok_sem,
     proj_sem,
     in_sem,
@@ -148,12 +172,21 @@
 
     for copy in in_copies + out_copies:
         copy.wait()
-    slot_out = jnp.zeros((slots, width), F32)
-    for c in range(FF_PARTS):
-        at = slice(c * ff_part, (c + 1) * ff_part)
-        hidden = jnp.dot(slot_in, w_in[:, at], preferred_element_type=F32)
-        hidden = jax.nn.gelu(hidden).astype(BF16)
-        slot_out = slot_out + jnp.dot(hidden, w_out[at, :], preferred_element_type=F32)
+    half = ff // 2
+    spread_slots(spread, slot_in.astype(F32))
+    hidden_m, hidden_v = [], []
+    for c in range(0, half, GROUP):
+        hidden_v.append(vector_dot(spread, w_in, 0, width, half + c))
+        hidden_m.append(jnp.dot(slot_in, w_in[:, c : c + GROUP], preferred_element_type=F32))
+    hidden_v = jax.nn.gelu(jnp.concatenate(hidden_v, axis=1)).astype(BF16)
+    hidden_m = jax.nn.gelu(jnp.concatenate(hidden_m, axis=1)).astype(BF16)
+    spread_slots(spread, hidden_v.astype(F32))
+    slot_out = []
+    for c in range(0, width, GROUP):
+        v = vector_dot(spread, w_out, half, half, c)
+        m = jnp.dot(hidden_m, w_out[:half, c : c + GROUP], preferred_element_type=F32)
+        slot_out.append(m + v)
+    slot_out = jnp.concatenate(slot_out, axis=1)
     gather[me] = slot_out.astype(BF16)
 
     second = []
@@ -220,6 +253,7 @@
             pltpu.VMEM((n - 1, slots, wide), BF16),
             pltpu.VMEM((n, slots, width), BF16),
             pltpu.VMEM((slots_all, width), F32),
+            pltpu.VMEM((slots, max(width, ff // 2), 128), BF16),
             dma((TOKEN_PARTS,)),
             dma,
             dma((FF_PARTS,)),

time: 23.4 us -> 23.1 us (0.987)
    pallas_call x1, Pallas kernels: 20.1 us -> 19.8 us  [body(): pl.pallas_call(functools.partial(route_kernel, n), out_shape=[jax.ShapeDt...]
where the time goes in v4:
time: 23.1 us; the launch traced here: 23 us
  Pallas kernels  23 us (100%)
    pallas_call x1, Pallas kernels, body(): pl.pallas_call(functools.partial(route_kernel, n), out_shape=[jax.ShapeDt...  19.8 us
    pallas_call x1, Pallas kernels, body(): pl.pallas_call(mix_kernel, out_shape=jax.ShapeDtypeStruct((count, width),...  3.16 us

profile of v4, /device:TPU:0, one launch (start us, length us, event | category | flops | bytes accessed | tf_op | source)
XLA Modules:
  0.0 23.0 jit_solution(4041398451397901797)
XLA Ops:
  0.0 19.8 %route.1 = (bf16[2560,16]{1,0:T(8,128)(2,1)S(1)}, bf16[16,1280]{1,0:T(8,128)(2,1)S(1)}) custom-call(bf16[2560,1280]{1,0:T(8,128)(2,1)} %tokens_hbm.1, bf16[16,1280]{1,0:T(8,128)(2,1)} %bitcast.1, bf16[1,1280,2560]{2,1,0:T(8,128)(2,1)} %w_in_hbm.1, bf16[1,2560,1280]{2,1,0:T(8,128)(2,1)} %w_out_hbm.1), custom_call_target="tpu_custom_call" | custom-call | flops 235929600 | bytes 19660800 | tf_op jit(solution)/shard_map/route/pallas_call | solution.py:238
  19.8 3.2 %mix.1 = bf16[2560,1280]{1,0:T(8,128)(2,1)} custom-call(bf16[2560,16]{1,0:T(8,128)(2,1)S(1)} %get-tuple-element.7.combine_ref, bf16[16,1280]{1,0:T(8,128)(2,1)S(1)} %get-tuple-element.8.slots_ref), custom_call_target="tpu_custom_call" | custom-call | flops 104857600 | bytes 6553600 | tf_op jit(solution)/shard_map/mix/pallas_call | solution.py:276

commit v5 on v4

--- a/solution.py
+++ b/solution.py
@@ -11,7 +11,6 @@
 F32 = jnp.float32
 BF16 = jnp.bfloat16
 TOKEN_PARTS = 5
-FF_PARTS = 5
 MIX_PARTS = 10
 GROUP = 256
 STAT = 128
@@ -77,7 +76,6 @@
     slots = send.shape[1]
     part = tok.shape[0] // TOKEN_PARTS
     ff = w_in.shape[1]
-    ff_part = ff // FF_PARTS
 
     proj_copy = pltpu.make_async_copy(proj_hbm, proj, proj_sem)
     proj_copy.start()
@@ -88,9 +86,10 @@
         copy.start()
         tok_copies.append(copy)
     in_copies, out_copies = [], []
-    for c in range(FF_PARTS):
-        at = pl.ds(c * ff_part, ff_part)
-        in_copies.append(pltpu.make_async_copy(w_in_hbm.at[0, :, at], w_in.at[:, at], in_sem.at[c]))
+    for c in range(TOKEN_PARTS):
+        at = pl.ds(c * (width // TOKEN_PARTS), width // TOKEN_PARTS)
+        in_copies.append(pltpu.make_async_copy(w_in_hbm.at[0, at, :], w_in.at[at, :], in_sem.at[c]))
+        at = pl.ds(c * (ff // TOKEN_PARTS), ff // TOKEN_PARTS)
         out_copies.append(pltpu.make_async_copy(w_out_hbm.at[0, at, :], w_out.at[at, :], out_sem.at[c]))
 
     barrier = pltpu.get_barrier_semaphore()
@@ -103,6 +102,8 @@
 
     def part_logits(c):
         tok_copies[c].wait()
+        in_copies[c].start()
+        out_copies[c].start()
         at = slice(c * part, (c + 1) * part)
         l = jnp.dot(tok[at, :], proj_cols, preferred_element_type=F32).T
         logits[:, at] = l
@@ -113,9 +114,6 @@
     for c in range(TOKEN_PARTS):
         if c + 1 < TOKEN_PARTS:
             following = part_logits(c + 1)
-            if c + 2 == TOKEN_PARTS:
-                for copy in in_copies + out_copies:
-                    copy.start()
         here = jnp.max(l, axis=1, keepdims=True)
         new = here if c == 0 else jnp.maximum(top, here)
         shifted = jnp.exp(l - new)
@@ -256,8 +254,8 @@
             pltpu.VMEM((slots, max(width, ff // 2), 128), BF16),
             dma((TOKEN_PARTS,)),
             dma,
-            dma((FF_PARTS,)),
-            dma((FF_PARTS,)),
+            dma((TOKEN_PARTS,)),
+            dma((TOKEN_PARTS,)),
             dma((n - 1,)),
             dma((n - 1,)),
             dma((n - 1,)),

time: 23.1 us -> 22.4 us (0.970)
  Pallas kernels: 23 us -> 22.2 us
    pallas_call x1, Pallas kernels: 19.8 us -> 19 us  [body(): pl.pallas_call(functools.partial(route_kernel, n), out_shape=[jax.ShapeDt...]
where the time goes in v5:
time: 22.4 us; the launch traced here: 22.2 us
  Pallas kernels  22.2 us (99%)
    pallas_call x1, Pallas kernels, body(): pl.pallas_call(functools.partial(route_kernel, n), out_shape=[jax.ShapeDt...  19 us
    pallas_call x1, Pallas kernels, body(): pl.pallas_call(mix_kernel, out_shape=jax.ShapeDtypeStruct((count, width),...  3.16 us

profile of v5, /device:TPU:0, one launch (start us, length us, event | category | flops | bytes accessed | tf_op | source)
XLA Modules:
  0.0 22.2 jit_solution(11670679130159749144)
XLA Ops:
  0.0 19.0 %route.1 = (bf16[2560,16]{1,0:T(8,128)(2,1)S(1)}, bf16[16,1280]{1,0:T(8,128)(2,1)S(1)}) custom-call(bf16[2560,1280]{1,0:T(8,128)(2,1)} %tokens_hbm.1, bf16[16,1280]{1,0:T(8,128)(2,1)} %bitcast.1, bf16[1,1280,2560]{2,1,0:T(8,128)(2,1)} %w_in_hbm.1, bf16[1,2560,1280]{2,1,0:T(8,128)(2,1)} %w_out_hbm.1), custom_call_target="tpu_custom_call" | custom-call | flops 235929600 | bytes 19660800 | tf_op jit(solution)/shard_map/route/pallas_call | solution.py:236
  19.0 3.2 %mix.1 = bf16[2560,1280]{1,0:T(8,128)(2,1)} custom-call(bf16[2560,16]{1,0:T(8,128)(2,1)S(1)} %get-tuple-element.7.combine_ref, bf16[16,1280]{1,0:T(8,128)(2,1)S(1)} %get-tuple-element.8.slots_ref), custom_call_target="tpu_custom_call" | custom-call | flops 104857600 | bytes 6553600 | tf_op jit(solution)/shard_map/mix/pallas_call | solution.py:274

commit v6 on v5

--- a/solution.py
+++ b/solution.py
@@ -98,14 +98,15 @@
         pl.semaphore_signal(barrier, inc=1, device_id={"seq": peer}, device_id_type=MESH)
 
     proj_copy.wait()
-    proj_cols = proj[...].T
 
     def part_logits(c):
         tok_copies[c].wait()
         in_copies[c].start()
         out_copies[c].start()
         at = slice(c * part, (c + 1) * part)
-        l = jnp.dot(tok[at, :], proj_cols, preferred_element_type=F32).T
+        l = lax.dot_general(
+            proj[...], tok[at, :], (((1,), (1,)), ((), ())), preferred_element_type=F32
+        )
         logits[:, at] = l
         return l
 

time: 22.4 us -> 20.9 us (0.933)
  Pallas kernels: 22.2 us -> 20.8 us
    pallas_call x1, Pallas kernels: 19 us -> 17.6 us  [body(): pl.pallas_call(functools.partial(route_kernel, n), out_shape=[jax.ShapeDt...]
where the time goes in v6:
time: 20.9 us; the launch traced here: 20.8 us
  Pallas kernels  20.8 us (100%)
    pallas_call x1, Pallas kernels, body(): pl.pallas_call(functools.partial(route_kernel, n), out_shape=[jax.ShapeDt...  17.6 us
    pallas_call x1, Pallas kernels, body(): pl.pallas_call(mix_kernel, out_shape=jax.ShapeDtypeStruct((count, width),...  3.16 us

profile of v6, /device:TPU:0, one launch (start us, length us, event | category | flops | bytes accessed | tf_op | source)
XLA Modules:
  0.0 20.8 jit_solution(12850348472940236388)
XLA Ops:
  0.0 17.6 %route.1 = (bf16[2560,16]{1,0:T(8,128)(2,1)S(1)}, bf16[16,1280]{1,0:T(8,128)(2,1)S(1)}) custom-call(bf16[2560,1280]{1,0:T(8,128)(2,1)} %tokens_hbm.1, bf16[16,1280]{1,0:T(8,128)(2,1)} %bitcast.1, bf16[1,1280,2560]{2,1,0:T(8,128)(2,1)} %w_in_hbm.1, bf16[1,2560,1280]{2,1,0:T(8,128)(2,1)} %w_out_hbm.1), custom_call_target="tpu_custom_call" | custom-call | flops 235929600 | bytes 19660800 | tf_op jit(solution)/shard_map/route/pallas_call | solution.py:237
  17.6 3.2 %mix.1 = bf16[2560,1280]{1,0:T(8,128)(2,1)} custom-call(bf16[2560,16]{1,0:T(8,128)(2,1)S(1)} %get-tuple-element.7.combine_ref, bf16[16,1280]{1,0:T(8,128)(2,1)S(1)} %get-tuple-element.8.slots_ref), custom_call_target="tpu_custom_call" | custom-call | flops 104857600 | bytes 6553600 | tf_op jit(solution)/shard_map/mix/pallas_call | solution.py:275

commit v7 on v3

--- a/solution.py
+++ b/solution.py
@@ -11,8 +11,8 @@
 F32 = jnp.float32
 BF16 = jnp.bfloat16
 TOKEN_PARTS = 5
-FF_PARTS = 5
 MIX_PARTS = 10
+FF_PART = 512
 STAT = 128
 
 
@@ -53,7 +53,6 @@
     slots = send.shape[1]
     part = tok.shape[0] // TOKEN_PARTS
     ff = w_in.shape[1]
-    ff_part = ff // FF_PARTS
 
     proj_copy = pltpu.make_async_copy(proj_hbm, proj, proj_sem)
     proj_copy.start()
@@ -64,9 +63,10 @@
         copy.start()
         tok_copies.append(copy)
     in_copies, out_copies = [], []
-    for c in range(FF_PARTS):
-        at = pl.ds(c * ff_part, ff_part)
-        in_copies.append(pltpu.make_async_copy(w_in_hbm.at[0, :, at], w_in.at[:, at], in_sem.at[c]))
+    for c in range(TOKEN_PARTS):
+        at = pl.ds(c * (width // TOKEN_PARTS), width // TOKEN_PARTS)
+        in_copies.append(pltpu.make_async_copy(w_in_hbm.at[0, at, :], w_in.at[at, :], in_sem.at[c]))
+        at = pl.ds(c * (ff // TOKEN_PARTS), ff // TOKEN_PARTS)
         out_copies.append(pltpu.make_async_copy(w_out_hbm.at[0, at, :], w_out.at[at, :], out_sem.at[c]))
 
     barrier = pltpu.get_barrier_semaphore()
@@ -75,12 +75,15 @@
         pl.semaphore_signal(barrier, inc=1, device_id={"seq": peer}, device_id_type=MESH)
 
     proj_copy.wait()
-    proj_cols = proj[...].T
 
     def part_logits(c):
         tok_copies[c].wait()
+        in_copies[c].start()
+        out_copies[c].start()
         at = slice(c * part, (c + 1) * part)
-        l = jnp.dot(tok[at, :], proj_cols, preferred_element_type=F32).T
+        l = lax.dot_general(
+            proj[...], tok[at, :], (((1,), (1,)), ((), ())), preferred_element_type=F32
+        )
         logits[:, at] = l
         return l
 
@@ -89,9 +92,6 @@
     for c in range(TOKEN_PARTS):
         if c + 1 < TOKEN_PARTS:
             following = part_logits(c + 1)
-            if c + 2 == TOKEN_PARTS:
-                for copy in in_copies + out_copies:
-                    copy.start()
         here = jnp.max(l, axis=1, keepdims=True)
         new = here if c == 0 else jnp.maximum(top, here)
         shifted = jnp.exp(l - new)
@@ -148,12 +148,18 @@
 
     for copy in in_copies + out_copies:
         copy.wait()
+    def first_product(c):
+        h = jnp.dot(slot_in, w_in[:, c : c + FF_PART], preferred_element_type=F32)
+        return jax.nn.gelu(h).astype(BF16)
+
     slot_out = jnp.zeros((slots, width), F32)
-    for c in range(FF_PARTS):
-        at = slice(c * ff_part, (c + 1) * ff_part)
-        hidden = jnp.dot(slot_in, w_in[:, at], preferred_element_type=F32)
-        hidden = jax.nn.gelu(hidden).astype(BF16)
-        slot_out = slot_out + jnp.dot(hidden, w_out[at, :], preferred_element_type=F32)
+    hidden = first_product(0)
+    for c in range(0, ff, FF_PART):
+        later = first_product(c + FF_PART) if c + FF_PART < ff else None
+        slot_out = slot_out + jnp.dot(
+            hidden, w_out[c : c + FF_PART, :], preferred_element_type=F32
+        )
+        hidden = later
     gather[me] = slot_out.astype(BF16)
 
     second = []
@@ -222,8 +228,8 @@
             pltpu.VMEM((slots_all, width), F32),
             dma((TOKEN_PARTS,)),
             dma,
-            dma((FF_PARTS,)),
-            dma((FF_PARTS,)),
+            dma((TOKEN_PARTS,)),
+            dma((TOKEN_PARTS,)),
             dma((n - 1,)),
             dma((n - 1,)),
             dma((n - 1,)),

time: 23.4 us -> 21 us (0.90)
  Pallas kernels: 23.2 us -> 20.8 us
    pallas_call x1, Pallas kernels: 20.1 us -> 17.7 us  [body(): pl.pallas_call(functools.partial(route_kernel, n), out_shape=[jax.ShapeDt...]
where the time goes in v7:
time: 21 us; the launch traced here: 20.8 us
  Pallas kernels  20.8 us (99%)
    pallas_call x1, Pallas kernels, body(): pl.pallas_call(functools.partial(route_kernel, n), out_shape=[jax.ShapeDt...  17.7 us
    pallas_call x1, Pallas kernels, body(): pl.pallas_call(mix_kernel, out_shape=jax.ShapeDtypeStruct((count, width),...  3.16 us

profile of v7, /device:TPU:0, one launch (start us, length us, event | category | flops | bytes accessed | tf_op | source)
XLA Modules:
  0.0 20.8 jit_solution(11387060998361683500)
XLA Ops:
  0.0 17.7 %route.1 = (bf16[2560,16]{1,0:T(8,128)(2,1)S(1)}, bf16[16,1280]{1,0:T(8,128)(2,1)S(1)}) custom-call(bf16[2560,1280]{1,0:T(8,128)(2,1)} %tokens_hbm.1, bf16[16,1280]{1,0:T(8,128)(2,1)} %bitcast.1, bf16[1,1280,2560]{2,1,0:T(8,128)(2,1)} %w_in_hbm.1, bf16[1,2560,1280]{2,1,0:T(8,128)(2,1)} %w_out_hbm.1), custom_call_target="tpu_custom_call" | custom-call | flops 235929600 | bytes 19660800 | tf_op jit(solution)/shard_map/route/pallas_call | solution.py:211
  17.7 3.2 %mix.1 = bf16[2560,1280]{1,0:T(8,128)(2,1)} custom-call(bf16[2560,16]{1,0:T(8,128)(2,1)S(1)} %get-tuple-element.7.combine_ref, bf16[16,1280]{1,0:T(8,128)(2,1)S(1)} %get-tuple-element.8.slots_ref), custom_call_target="tpu_custom_call" | custom-call | flops 104857600 | bytes 6553600 | tf_op jit(solution)/shard_map/mix/pallas_call | solution.py:248

commit v8 on v7

--- a/solution.py
+++ b/solution.py
@@ -12,7 +12,6 @@
 BF16 = jnp.bfloat16
 TOKEN_PARTS = 5
 MIX_PARTS = 10
-FF_PART = 512
 STAT = 128
 
 
@@ -78,8 +77,8 @@
 
     def part_logits(c):
         tok_copies[c].wait()
-        in_copies[c].start()
-        out_copies[c].start()
+        for copy in (in_copies + out_copies)[2 * c : 2 * c + 2]:
+            copy.start()
         at = slice(c * part, (c + 1) * part)
         l = lax.dot_general(
             proj[...], tok[at, :], (((1,), (1,)), ((), ())), preferred_element_type=F32
@@ -146,20 +145,17 @@
         num = num + scale * got[k][:, :width]
     slot_in = (num / total).astype(BF16)
 
-    for copy in in_copies + out_copies:
-        copy.wait()
-    def first_product(c):
-        h = jnp.dot(slot_in, w_in[:, c : c + FF_PART], preferred_element_type=F32)
-        return jax.nn.gelu(h).astype(BF16)
-
+    hidden = jnp.zeros((slots, ff), F32)
+    for c in range(TOKEN_PARTS):
+        at = slice(c * (width // TOKEN_PARTS), (c + 1) * (width // TOKEN_PARTS))
+        in_copies[c].wait()
+        hidden = hidden + jnp.dot(slot_in[:, at], w_in[at, :], preferred_element_type=F32)
+    hidden = jax.nn.gelu(hidden).astype(BF16)
     slot_out = jnp.zeros((slots, width), F32)
-    hidden = first_product(0)
-    for c in range(0, ff, FF_PART):
-        later = first_product(c + FF_PART) if c + FF_PART < ff else None
-        slot_out = slot_out + jnp.dot(
-            hidden, w_out[c : c + FF_PART, :], preferred_element_type=F32
-        )
-        hidden = later
+    for c in range(TOKEN_PARTS):
+        at = slice(c * (ff // TOKEN_PARTS), (c + 1) * (ff // TOKEN_PARTS))
+        out_copies[c].wait()
+        slot_out = slot_out + jnp.dot(hidden[:, at], w_out[at, :], preferred_element_type=F32)
     gather[me] = slot_out.astype(BF16)
 
     second = []

time: 21 us -> 22.6 us (1.076)
  Pallas kernels: 20.8 us -> 22.5 us
    pallas_call x1, Pallas kernels: 17.7 us -> 19.3 us  [body(): pl.pallas_call(functools.partial(route_kernel, n), out_shape=[jax.ShapeDt...]
where the time goes in v8:
time: 22.6 us; the launch traced here: 22.5 us
  Pallas kernels  22.5 us (100%)
    pallas_call x1, Pallas kernels, body(): pl.pallas_call(functools.partial(route_kernel, n), out_shape=[jax.ShapeDt...  19.3 us
    pallas_call x1, Pallas kernels, body(): pl.pallas_call(mix_kernel, out_shape=jax.ShapeDtypeStruct((count, width),...  3.16 us

profile of v8, /device:TPU:0, one launch (start us, length us, event | category | flops | bytes accessed | tf_op | source)
XLA Modules:
  0.0 22.5 jit_solution(13316413965766349189)
XLA Ops:
  0.0 19.3 %route.1 = (bf16[2560,16]{1,0:T(8,128)(2,1)S(1)}, bf16[16,1280]{1,0:T(8,128)(2,1)S(1)}) custom-call(bf16[2560,1280]{1,0:T(8,128)(2,1)} %tokens_hbm.1, bf16[16,1280]{1,0:T(8,128)(2,1)} %bitcast.1, bf16[1,1280,2560]{2,1,0:T(8,128)(2,1)} %w_in_hbm.1, bf16[1,2560,1280]{2,1,0:T(8,128)(2,1)} %w_out_hbm.1), custom_call_target="tpu_custom_call" | custom-call | flops 235929600 | bytes 19660800 | tf_op jit(solution)/shard_map/route/pallas_call | solution.py:207
  19.3 3.2 %mix.1 = bf16[2560,1280]{1,0:T(8,128)(2,1)} custom-call(bf16[2560,16]{1,0:T(8,128)(2,1)S(1)} %get-tuple-element.7.combine_ref, bf16[16,1280]{1,0:T(8,128)(2,1)S(1)} %get-tuple-element.8.slots_ref), custom_call_target="tpu_custom_call" | custom-call | flops 104857600 | bytes 6553600 | tf_op jit(solution)/shard_map/mix/pallas_call | solution.py:244

commit v9 on v6

--- a/solution.py
+++ b/solution.py
@@ -11,7 +11,8 @@
 F32 = jnp.float32
 BF16 = jnp.bfloat16
 TOKEN_PARTS = 5
-MIX_PARTS = 10
+MIX_PARTS = 20
+VECTOR_FF = 768
 GROUP = 256
 STAT = 128
 
@@ -171,19 +172,20 @@
 
     for copy in in_copies + out_copies:
         copy.wait()
-    half = ff // 2
+    split = ff - VECTOR_FF
     spread_slots(spread, slot_in.astype(F32))
     hidden_m, hidden_v = [], []
-    for c in range(0, half, GROUP):
-        hidden_v.append(vector_dot(spread, w_in, 0, width, half + c))
+    for c in range(0, split, GROUP):
+        if c < VECTOR_FF:
+            hidden_v.append(vector_dot(spread, w_in, 0, width, split + c))
         hidden_m.append(jnp.dot(slot_in, w_in[:, c : c + GROUP], preferred_element_type=F32))
     hidden_v = jax.nn.gelu(jnp.concatenate(hidden_v, axis=1)).astype(BF16)
     hidden_m = jax.nn.gelu(jnp.concatenate(hidden_m, axis=1)).astype(BF16)
     spread_slots(spread, hidden_v.astype(F32))
     slot_out = []
     for c in range(0, width, GROUP):
-        v = vector_dot(spread, w_out, half, half, c)
-        m = jnp.dot(hidden_m, w_out[:half, c : c + GROUP], preferred_element_type=F32)
+        v = vector_dot(spread, w_out, split, VECTOR_FF, c)
+        m = jnp.dot(hidden_m, w_out[:split, c : c + GROUP], preferred_element_type=F32)
         slot_out.append(m + v)
     slot_out = jnp.concatenate(slot_out, axis=1)
     gather[me] = slot_out.astype(BF16)
@@ -252,7 +254,7 @@
             pltpu.VMEM((n - 1, slots, wide), BF16),
             pltpu.VMEM((n, slots, width), BF16),
             pltpu.VMEM((slots_all, width), F32),
-            pltpu.VMEM((slots, max(width, ff // 2), 128), BF16),
+            pltpu.VMEM((slots, max(width, VECTOR_FF), 128), BF16),
             dma((TOKEN_PARTS,)),
             dma,
             dma((TOKEN_PARTS,)),

time: 20.9 us -> 20.7 us (level)
  no operation moved by 1% of the time
where the time goes in v9:
time: 20.7 us; the launch traced here: 20.6 us
  Pallas kernels  20.6 us (100%)
    pallas_call x1, Pallas kernels, body(): pl.pallas_call(functools.partial(route_kernel, n), out_shape=[jax.ShapeDt...  17.5 us
    pallas_call x1, Pallas kernels, body(): pl.pallas_call(mix_kernel, out_shape=jax.ShapeDtypeStruct((count, width),...  3.12 us

profile of v9, /device:TPU:0, one launch (start us, length us, event | category | flops | bytes accessed | tf_op | source)
XLA Modules:
  0.0 20.6 jit_solution(17351021162065955595)
XLA Ops:
  0.0 17.5 %route.1 = (bf16[2560,16]{1,0:T(8,128)(2,1)S(1)}, bf16[16,1280]{1,0:T(8,128)(2,1)S(1)}) custom-call(bf16[2560,1280]{1,0:T(8,128)(2,1)} %tokens_hbm.1, bf16[16,1280]{1,0:T(8,128)(2,1)} %bitcast.1, bf16[1,1280,2560]{2,1,0:T(8,128)(2,1)} %w_in_hbm.1, bf16[1,2560,1280]{2,1,0:T(8,128)(2,1)} %w_out_hbm.1), custom_call_target="tpu_custom_call" | custom-call | flops 235929600 | bytes 19660800 | tf_op jit(solution)/shard_map/route/pallas_call | solution.py:239
  17.5 3.1 %mix.1 = bf16[2560,1280]{1,0:T(8,128)(2,1)} custom-call(bf16[2560,16]{1,0:T(8,128)(2,1)S(1)} %get-tuple-element.7.combine_ref, bf16[16,1280]{1,0:T(8,128)(2,1)S(1)} %get-tuple-element.8.slots_ref), custom_call_target="tpu_custom_call" | custom-call | flops 104857600 | bytes 6553600 | tf_op jit(solution)/shard_map/mix/pallas_call | solution.py:277

commit v10 on v9

--- a/solution.py
+++ b/solution.py
@@ -10,7 +10,9 @@
 MESH = pl.DeviceIdType.MESH
 F32 = jnp.float32
 BF16 = jnp.bfloat16
-TOKEN_PARTS = 5
+TOKEN_CUTS = (0, 1, 3, 5)
+TOKEN_PARTS = len(TOKEN_CUTS) - 1
+WEIGHT_PARTS = 5
 MIX_PARTS = 20
 VECTOR_FF = 768
 GROUP = 256
@@ -75,22 +77,22 @@
     me = lax.axis_index("seq")
     width = tok.shape[1]
     slots = send.shape[1]
-    part = tok.shape[0] // TOKEN_PARTS
+    cuts = [c * (tok.shape[0] // TOKEN_CUTS[-1]) for c in TOKEN_CUTS]
     ff = w_in.shape[1]
 
     proj_copy = pltpu.make_async_copy(proj_hbm, proj, proj_sem)
     proj_copy.start()
     tok_copies = []
     for c in range(TOKEN_PARTS):
-        at = pl.ds(c * part, part)
+        at = pl.ds(cuts[c], cuts[c + 1] - cuts[c])
         copy = pltpu.make_async_copy(tokens_hbm.at[at, :], tok.at[at, :], tok_sem.at[c])
         copy.start()
         tok_copies.append(copy)
     in_copies, out_copies = [], []
-    for c in range(TOKEN_PARTS):
-        at = pl.ds(c * (width // TOKEN_PARTS), width // TOKEN_PARTS)
+    for c in range(WEIGHT_PARTS):
+        at = pl.ds(c * (width // WEIGHT_PARTS), width // WEIGHT_PARTS)
         in_copies.append(pltpu.make_async_copy(w_in_hbm.at[0, at, :], w_in.at[at, :], in_sem.at[c]))
-        at = pl.ds(c * (ff // TOKEN_PARTS), ff // TOKEN_PARTS)
+        at = pl.ds(c * (ff // WEIGHT_PARTS), ff // WEIGHT_PARTS)
         out_copies.append(pltpu.make_async_copy(w_out_hbm.at[0, at, :], w_out.at[at, :], out_sem.at[c]))
 
     barrier = pltpu.get_barrier_semaphore()
@@ -102,9 +104,10 @@
 
     def part_logits(c):
         tok_copies[c].wait()
-        in_copies[c].start()
-        out_copies[c].start()
-        at = slice(c * part, (c + 1) * part)
+        begun = slice(TOKEN_CUTS[c], TOKEN_CUTS[c + 1])
+        for copy in in_copies[begun] + out_copies[begun]:
+            copy.start()
+        at = slice(cuts[c], cuts[c + 1])
         l = lax.dot_general(
             proj[...], tok[at, :], (((1,), (1,)), ((), ())), preferred_element_type=F32
         )
@@ -120,7 +123,7 @@
         new = here if c == 0 else jnp.maximum(top, here)
         shifted = jnp.exp(l - new)
         t = jnp.sum(shifted, axis=1, keepdims=True)
-        x = tok[c * part : (c + 1) * part, :]
+        x = tok[cuts[c] : cuts[c + 1], :]
         v = jnp.dot(shifted.astype(BF16), x, preferred_element_type=F32)
         if c == 0:
             total, num = t, v
@@ -257,8 +260,8 @@
             pltpu.VMEM((slots, max(width, VECTOR_FF), 128), BF16),
             dma((TOKEN_PARTS,)),
             dma,
-            dma((TOKEN_PARTS,)),
-            dma((TOKEN_PARTS,)),
+            dma((WEIGHT_PARTS,)),
+            dma((WEIGHT_PARTS,)),
             dma((n - 1,)),
             dma((n - 1,)),
             dma((n - 1,)),

time: 20.7 us -> 20 us (0.966)
  Pallas kernels: 20.6 us -> 19.8 us
    pallas_call x1, Pallas kernels: 17.5 us -> 16.7 us  [body(): pl.pallas_call(functools.partial(route_kernel, n), out_shape=[jax.ShapeDt...]
where the time goes in v10:
time: 20 us; the launch traced here: 19.9 us
  Pallas kernels  19.8 us (99%)
    pallas_call x1, Pallas kernels, body(): pl.pallas_call(functools.partial(route_kernel, n), out_shape=[jax.ShapeDt...  16.7 us
    pallas_call x1, Pallas kernels, body(): pl.pallas_call(mix_kernel, out_shape=jax.ShapeDtypeStruct((count, width),...  3.12 us

profile of v10, /device:TPU:0, one launch (start us, length us, event | category | flops | bytes accessed | tf_op | source)
XLA Modules:
  0.0 19.9 jit_solution(18183656223006143290)
XLA Ops:
  0.0 16.7 %route.1 = (bf16[2560,16]{1,0:T(8,128)(2,1)S(1)}, bf16[16,1280]{1,0:T(8,128)(2,1)S(1)}) custom-call(bf16[2560,1280]{1,0:T(8,128)(2,1)} %tokens_hbm.1, bf16[16,1280]{1,0:T(8,128)(2,1)} %bitcast.1, bf16[1,1280,2560]{2,1,0:T(8,128)(2,1)} %w_in_hbm.1, bf16[1,2560,1280]{2,1,0:T(8,128)(2,1)} %w_out_hbm.1), custom_call_target="tpu_custom_call" | custom-call | flops 235929600 | bytes 19660800 | tf_op jit(solution)/shard_map/route/pallas_call | solution.py:242
  16.7 3.1 %mix.1 = bf16[2560,1280]{1,0:T(8,128)(2,1)} custom-call(bf16[2560,16]{1,0:T(8,128)(2,1)S(1)} %get-tuple-element.7.combine_ref, bf16[16,1280]{1,0:T(8,128)(2,1)S(1)} %get-tuple-element.8.slots_ref), custom_call_target="tpu_custom_call" | custom-call | flops 104857600 | bytes 6553600 | tf_op jit(solution)/shard_map/mix/pallas_call | solution.py:280
